TPU v7x, 256 devices: a whole 4x4x8 slice. The times are simulated.
256 devices in a mesh: ao: 16 (over x, y_hi, core), aux: 16 (over y_lo, z).
Axes of the slice: x: 4, y: 4 (y_hi: 2, y_lo: 2; y = y_hi * 2 + y_lo), z: 8, core: 2. Of those that a mesh axis runs over, the one named last changes fastest.
Arguments:
- orbital_factors: float32 [32, 500, 10240], P('aux', None, 'ao'), may hold values from -1.75 to 1.75
- plan: int32 [2, 16], replicated, may hold values from 0 to 15, as said below
Outputs:
- exchange_tiles: float32 [2, 10240, 640], P(None, ('ao', 'aux'))
Inputs may be any that keep to these rules, and one draw needn't show every extreme that they name: `plan`: in round r every block a has the partner a XOR s_r, with one nonzero s_r for each round and different s_r in different rounds.
All inputs are finite; a program needn't handle non-finite values.
Results may differ from a plain program's by a relative error of at most 0.0003.
Values sent between devices are 32-bit elements; how exact they have to be, the bound alone decides.
No kernel may reach another device: no remote copies, remote signals or barrier semaphores. Data moves between devices by JAX's collectives and lax.ppermute only.
A program may use at most 64 MiB of HBM per device.

v0:
```python
import jax
import jax.numpy as jnp
from jax import lax
from jax.sharding import PartitionSpec as P


def partner_2(block, axis, apart):
    count = lax.axis_size(axis)
    route = []
    for low in range(count):
        high = low | 1 << apart
        if high != low and high < count:
            route += [(low, high), (high, low)]
    return lax.ppermute(block, axis, route)


def local(orbital_factors, plan):
    flat_rows = orbital_factors.reshape(-1, orbital_factors.shape[2])
    block_index = lax.axis_index("ao")
    count_bits = lax.axis_size("ao").bit_length() - 1
    bit_list = list(range(count_bits))
    partials = []
    for step in range(plan.shape[0]):
        partner = lax.dynamic_index_in_dim(plan[step], block_index, 0, keepdims=False)
        partner_mask = jnp.bitwise_xor(partner, block_index)
        holder = flat_rows
        for bit in bit_list:
            bit_set = jnp.right_shift(partner_mask, bit) % 2 == 1
            moved = partner_2(holder, "ao", bit)
            holder = jnp.where(bit_set, moved, holder)
        partial_tile = lax.dot_general(
            flat_rows,
            holder,
            (((0,), (0,)), ((), ())),
            precision=lax.Precision.HIGHEST,
            preferred_element_type=jnp.float32,
        )
        partials.append(lax.psum_scatter(partial_tile, "aux", scatter_dimension=0, tiled=True))
    return jnp.stack(partials, 0)


def solution(mesh):
    placed = (P("aux", None, "ao"), P())
    return jax.shard_map(
        local, mesh=mesh, in_specs=placed, out_specs=P(None, ("ao", "aux"), None), check_vma=False
    )
```

profile of v0, /device:TPU:1, one launch (start us, length us, event | category | flops | bytes accessed | tf_op | source)
XLA Modules:
  0.0 469.7 jit_solution(7117961113330186765)
XLA Ops:
  6.5 0.0 all-reduce.5.cloned.1.call-start
  6.5 3.4 copy.6
  9.9 0.0 copy-start
  9.9 2.0 reshape.7
  11.9 3.3 collective-permute-start
  15.3 0.0 copy-done
  15.3 0.6 constant_dynamic-slice_fusion
  17.2 2.6 collective-permute-done
  19.8 4.3 broadcast_select_fusion.3
  24.2 1.2 collective-permute-start.1
  25.3 1.8 collective-permute-start.4
  27.1 55.6 %collective-permute-done.1 = f32[1000,640]{1,0:T(8,128)} collective-permute-done((f32[1000,640]{1,0:T(8,128)}, f32[1000,640]{1,0:T(8,128)}, u32[]{:S(2)}, u32[]{:S(2)}) %collective-permute-start.1) | collective-permute-done | bytes 2560032 | tf_op jit(solution)/shard_map/ppermute | solution.py:14
  82.7 3.5 broadcast_select_fusion.4
  86.2 0.0 collective-permute-start.2
  86.2 51.4 %collective-permute-done.4 = f32[1000,640]{1,0:T(8,128)} collective-permute-done((f32[1000,640]{1,0:T(8,128)}, f32[1000,640]{1,0:T(8,128)}, u32[]{:S(2)}, u32[]{:S(2)}) %collective-permute-start.4) | collective-permute-done | bytes 2560032 | tf_op jit(solution)/shard_map/ppermute | solution.py:14
  137.6 3.5 broadcast_select_fusion.1
  141.1 0.0 collective-permute-start.5
  141.1 0.5 collective-permute-done.2
  141.6 3.5 broadcast_select_fusion.5
  145.0 1.4 collective-permute-start.3
  146.4 50.8 %collective-permute-done.5 = f32[1000,640]{1,0:T(8,128)} collective-permute-done((f32[1000,640]{1,0:T(8,128)}, f32[1000,640]{1,0:T(8,128)}, u32[]{:S(2)}, u32[]{:S(2)}) %collective-permute-start.5) | collective-permute-done | bytes 2560032 | tf_op jit(solution)/shard_map/ppermute | solution.py:14
  197.2 3.5 broadcast_select_fusion.2
  200.7 1.0 collective-permute-start.6
  201.7 50.8 %collective-permute-done.3 = f32[1000,640]{1,0:T(8,128)} collective-permute-done((f32[1000,640]{1,0:T(8,128)}, f32[1000,640]{1,0:T(8,128)}, u32[]{:S(2)}, u32[]{:S(2)}) %collective-permute-start.3) | collective-permute-done | bytes 2560032 | tf_op jit(solution)/shard_map/ppermute | solution.py:14
  252.5 9.4 %fusion.4 = f32[640,640]{0,1:T(8,128)} fusion(f32[1000,640]{1,0:T(8,128)S(1)} %reshape.7, f32[1000,640]{1,0:T(8,128)} %collective-permute-done.3, f32[1000,640]{1,0:T(8,128)} %broadcast_select_fusion.5, pred[]{:T(512)S(6)} %eq.33), kind=kOutput, calls=%fused_computation.4 | convolution fusion | flops 4915840000 | bytes 9318401 | tf_op jit(solution)/shard_map/dot_general | solution.py:31
  262.0 45.4 %collective-permute-done.6 = f32[1000,640]{1,0:T(8,128)} collective-permute-done((f32[1000,640]{1,0:T(8,128)}, f32[1000,640]{1,0:T(8,128)}, u32[]{:S(2)}, u32[]{:S(2)}) %collective-permute-start.6) | collective-permute-done | bytes 2560032 | tf_op jit(solution)/shard_map/ppermute | solution.py:14
  307.4 9.5 %fusion.7 = f32[640,640]{0,1:T(8,128)} fusion(f32[1000,640]{1,0:T(8,128)S(1)} %reshape.7, f32[1000,640]{1,0:T(8,128)} %collective-permute-done.6, f32[1000,640]{1,0:T(8,128)} %broadcast_select_fusion.2, pred[]{:T(512)S(6)} %eq.37), kind=kOutput, calls=%fused_computation.5 | convolution fusion | flops 4915840000 | bytes 9318401 | tf_op jit(solution)/shard_map/dot_general | solution.py:31
  316.9 0.0 copy-start.1
  316.9 0.0 all-reduce.5.cloned.1.call-update
  316.9 0.6 copy-done.1
  317.6 0.6 dynamic-slice.2
  318.8 140.5 %all-reduce.5.cloned.1.call-done = (f32[640,640]{0,1:T(8,128)}, f32[640,640]{0,1:T(8,128)}) async-done(((f32[640,640]{0,1:T(8,128)}, f32[640,640]{0,1:T(8,128)}), (f32[640,640]{0,1:T(8,128)}, f32[640,640]{0,1:T(8,128)})) %all-reduce.5.cloned.1.call-update) | async-done | bytes 3276816
  459.4 1.2 dynamic-slice_bitcast_fusion.1
  460.6 0.1 copy.7
  460.7 1.2 dynamic-slice_bitcast_fusion
  462.0 0.1 copy.8
  462.1 0.7 pad_maximum_fusion
  (1 shorter events, 0.0 us)
Async XLA Ops:
  6.5 452.8 %all-reduce.5.cloned.1.call-start = ((), (), s32[]{:S(2)}) async-start(), calls=%async_computation | async-start | bytes 6553600
  9.9 5.3 %copy-start = (s32[2,16]{1,0:T(2,128)S(1)}, s32[2,16]{1,0:T(2,128)}, u32[]{:S(2)}) copy-start(s32[2,16]{1,0:T(2,128)} %param.3) | copy-start | bytes 388
  11.9 7.9 %collective-permute-start = (f32[1000,640]{1,0:T(8,128)S(1)}, f32[1000,640]{1,0:T(8,128)}, u32[]{:S(2)}, u32[]{:S(2)}) collective-permute-start(f32[1000,640]{1,0:T(8,128)S(1)} %reshape.7), channel_id=1, source_target_pairs={{0,16},{16,0},{32,48},{48,32},{64,80},{80,64},{96,112},{112,96},{1... | collective-permute-start | bytes 7680008 | tf_op jit(solution)/shard_map/ppermute | solution.py:14
  24.2 58.6 %collective-permute-start.1 = (f32[1000,640]{1,0:T(8,128)}, f32[1000,640]{1,0:T(8,128)}, u32[]{:S(2)}, u32[]{:S(2)}) collective-permute-start(f32[1000,640]{1,0:T(8,128)} %get-tuple-element.7), channel_id=1, source_target_pairs={{0,32},{32,0},{16,48},{48,16},{64,96},{96,64},{80,112},{112,80},{1... | collective-permute-start | bytes 7680008 | tf_op jit(solution)/shard_map/ppermute | solution.py:14
  25.3 112.3 %collective-permute-start.4 = (f32[1000,640]{1,0:T(8,128)}, f32[1000,640]{1,0:T(8,128)}, u32[]{:S(2)}, u32[]{:S(2)}) collective-permute-start(f32[1000,640]{1,0:T(8,128)} %get-tuple-element.8), channel_id=1, source_target_pairs={{0,32},{32,0},{16,48},{48,16},{64,96},{96,64},{80,112},{112,80},{1... | collective-permute-start | bytes 7680008 | tf_op jit(solution)/shard_map/ppermute | solution.py:14
  86.2 55.4 %collective-permute-start.2 = (f32[1000,640]{1,0:T(8,128)}, f32[1000,640]{1,0:T(8,128)}, u32[]{:S(2)}, u32[]{:S(2)}) collective-permute-start(f32[1000,640]{1,0:T(8,128)} %broadcast_select_fusion.4), channel_id=1, source_target_pairs={{0,64},{64,0},{16,80},{80,16},{32,96},{96,32},{48,112},{112,48},{1... | collective-permute-start | bytes 7680008 | tf_op jit(solution)/shard_map/ppermute | solution.py:14
  141.1 56.2 %collective-permute-start.5 = (f32[1000,640]{1,0:T(8,128)}, f32[1000,640]{1,0:T(8,128)}, u32[]{:S(2)}, u32[]{:S(2)}) collective-permute-start(f32[1000,640]{1,0:T(8,128)} %broadcast_select_fusion.1), channel_id=1, source_target_pairs={{0,64},{64,0},{16,80},{80,16},{32,96},{96,32},{48,112},{112,48},{1... | collective-permute-start | bytes 7680008 | tf_op jit(solution)/shard_map/ppermute | solution.py:14
  145.0 107.5 %collective-permute-start.3 = (f32[1000,640]{1,0:T(8,128)}, f32[1000,640]{1,0:T(8,128)}, u32[]{:S(2)}, u32[]{:S(2)}) collective-permute-start(f32[1000,640]{1,0:T(8,128)} %broadcast_select_fusion.5), channel_id=1, source_target_pairs={{0,128},{128,0},{16,144},{144,16},{32,160},{160,32},{48,176},{176,... | collective-permute-start | bytes 7680008 | tf_op jit(solution)/shard_map/ppermute | solution.py:14
  200.7 106.7 %collective-permute-start.6 = (f32[1000,640]{1,0:T(8,128)}, f32[1000,640]{1,0:T(8,128)}, u32[]{:S(2)}, u32[]{:S(2)}) collective-permute-start(f32[1000,640]{1,0:T(8,128)} %broadcast_select_fusion.2), channel_id=1, source_target_pairs={{0,128},{128,0},{16,144},{144,16},{32,160},{160,32},{48,176},{176,... | collective-permute-start | bytes 7680008 | tf_op jit(solution)/shard_map/ppermute | solution.py:14
  316.9 0.7 copy-start.1
Sparse Core Ops, SparseCore 0:
  317.1 142.2 all-reduce.4
where the time goes:
time: 479 us; the launch traced here: 470 us
  waiting for transfers between devices  398 us (83%)
  matrix products  19 us (4%)
  other arithmetic  18.9 us (4%)
  between operations  15.4 us (3%)
  local copies, waits for them, and re-layouts  9.99 us (2%)
  starting transfers between devices  8.75 us (2%)
    ppermute x7, waiting for transfers between devices, partner_2(): return lax.ppermute(block, axis, route)  257 us
    unnamed x2, waiting for transfers between devices  141 us
    dot_general x2, matrix products, local(): lax.dot_general(flat_rows, holder, (((0,), (0,)), ((), ())), precision=la...  19 us
    select_n x5, other arithmetic, local(): holder = jnp.where(bit_set, moved, holder)  18.2 us
  transfers between devices with their start and end apart: 8, of which 8 were waited for; matrix products, arithmetic and copies ran while one was open for 5% of the time, Pallas kernels for 0%

commit v1 on v0

v1 whole, which is shorter than its diff:
```python
import jax
import jax.numpy as jnp
import numpy as np
from jax import lax
from jax.experimental import pallas as pl
from jax.experimental.pallas import tpu as pltpu
from jax.sharding import PartitionSpec as P

CHIPS = 8
SWAP = [(a, a ^ 1) for a in range(2 * CHIPS)]
DIMS = (((0,), (0,)), ((), ()))


def odd(value):
    return bin(value).count("1") & 1


def chip_split(low, high):
    if low >> 1 == high >> 1:
        return (low >> 1) & -(low >> 1)
    for split in range(CHIPS):
        if odd(split & (low >> 1)) == 1 ^ (low & 1) and odd(split & (high >> 1)) == 1 ^ (high & 1):
            return split


def split_table():
    table = np.zeros((2 * CHIPS, 2 * CHIPS), np.int32)
    for low in range(1, 2 * CHIPS):
        for high in range(low + 1, 2 * CHIPS):
            table[low, high] = chip_split(low, high)
    return table.reshape(-1)


def routes():
    out = []
    for high in range(1, CHIPS):
        for low in range(high):
            out.append([((d ^ (high if c else low)) * 2 + (c ^ 1), d * 2 + c) for d in range(CHIPS) for c in range(2)])
    for mask in range(1, CHIPS):
        split = mask & -mask
        out.append([((d ^ mask) * 2 + (c ^ odd(split & d)), d * 2 + c) for d in range(CHIPS) for c in range(2)])
    return out


def tile_kernel(a_ref, p_ref, o_ref, p_high, p_low):
    @pl.when(pl.program_id(0) == 0)
    def _():
        p = p_ref[...]
        high = p.astype(jnp.bfloat16)
        p_high[...] = high
        p_low[...] = (p - high.astype(jnp.float32)).astype(jnp.bfloat16)

    a = a_ref[...]
    high = a.astype(jnp.bfloat16)
    low = (a - high.astype(jnp.float32)).astype(jnp.bfloat16)
    total = None
    for left, right in ((low, p_high), (high, p_low), (high, p_high)):
        part = lax.dot_general(left, right[...], DIMS, preferred_element_type=jnp.float32)
        total = part if total is None else total + part
    o_ref[...] = total


def tile_of(block, partner):
    depth, width = block.shape
    rows = 128
    return pl.pallas_call(
        tile_kernel,
        grid=(width // rows,),
        out_shape=jax.ShapeDtypeStruct((width, width), jnp.float32),
        in_specs=[
            pl.BlockSpec((depth, rows), lambda i: (0, i)),
            pl.BlockSpec((depth, width), lambda i: (0, 0)),
        ],
        out_specs=pl.BlockSpec((rows, width), lambda i: (i, 0)),
        scratch_shapes=[pltpu.VMEM((depth, width), jnp.bfloat16)] * 2,
        compiler_params=pltpu.CompilerParams(vmem_limit_bytes=32 << 20),
    )(block, partner)


def local(orbital_factors, plan):
    parts = lax.axis_size("aux")
    own = lax.axis_index("ao")
    chip, core = own >> 1, own & 1
    low, high = jnp.min(plan[:, 0]), jnp.max(plan[:, 0])
    low_round = jnp.where(plan[0, 0] == low, 0, 1)
    low_chip, high_chip = low >> 1, high >> 1
    same = low_chip == high_chip
    split = jnp.asarray(split_table())[low * (2 * CHIPS) + high]
    side = lax.population_count(chip & split) & 1
    own_round = low_round ^ jnp.where(same, side, core ^ side)
    case = jnp.where(same, 27 + low_chip, (high_chip * (high_chip - 1) >> 1) + low_chip)
    mask = jnp.where(core == 1, high_chip, low_chip)

    width = orbital_factors.shape[2]
    rows = lax.optimization_barrier(jnp.swapaxes(orbital_factors, 0, 1).reshape(-1, width))
    sibling = lax.ppermute(rows, "ao", SWAP)
    block = lax.optimization_barrier(jnp.where((side == 1) & ~same, sibling, rows))
    partner = lax.switch(
        case, [lambda x, r=r: lax.ppermute(x, "ao", r) for r in routes()], block
    )
    tile = tile_of(block, partner)
    share = width // parts
    slabs = lax.all_to_all(tile.reshape(parts, share, width), "aux", 0, 0)
    mine = jnp.sum(slabs, 0)
    flipped = mine.T.reshape(parts, share, share)
    cross = lax.all_to_all(flipped, "aux", 0, 0)
    theirs = jnp.moveaxis(cross, 0, 1).reshape(share, width)
    for bit in range(3):
        moved = lax.ppermute(theirs, "ao", [(a, a ^ (2 << bit)) for a in range(2 * CHIPS)])
        theirs = jnp.where((mask >> bit) & 1 == 1, moved, theirs)
    sent = jnp.where(side == 1, mine, theirs)
    kept = jnp.where(side == 1, theirs, mine)
    got = lax.ppermute(sent, "ao", SWAP)
    got = jnp.where(same & (side == 1), sent, got)
    straight = own_round == side
    return jnp.stack([jnp.where(straight, kept, got), jnp.where(straight, got, kept)], 0)


def solution(mesh):
    placed = (P("aux", None, "ao"), P())
    return jax.shard_map(
        local, mesh=mesh, in_specs=placed, out_specs=P(None, ("ao", "aux"), None), check_vma=False
    )
```

time: 479 us -> 136 us (0.28); the launches traced: 470 us -> 135 us
  waiting for transfers between devices: 398 us -> 36.7 us
  blocking collectives: 0 us -> 57.8 us
  matrix products: 19 us -> 0 us
  other arithmetic: 18.9 us -> 2.68 us
  between operations: 15.4 us -> 4.6 us
  starting transfers between devices: 8.75 us -> 18.6 us
  Pallas kernels: 0 us -> 6.86 us
    ppermute x7 -> x6, waiting for transfers between devices: 257 us -> 36.7 us  [the longest x1 29.4 us: local(): lax.ppermute(x, 'ao', r)]
    unnamed x2 -> x0, waiting for transfers between devices: 141 us -> none
    all_to_all x0 -> x2, blocking collectives: none -> 57.8 us  [the longest x1 45.6 us: local(): slabs = lax.all_to_all(tile.reshape(parts, share, width), 'aux', 0, 0)]
    dot_general x2 -> x0, matrix products: 19 us -> none  [local(): lax.dot_general(flat_rows, holder, (((0,), (0,)), ((), ())), precision=la...]
    select_n x5 -> x4, other arithmetic: 18.2 us -> 0.32 us  [the longest x1 0.27 us: local(): jnp.where((side == 1) & ~same, sibling, rows)]
    ppermute x7 -> x6, starting transfers between devices: 8.75 us -> 18.6 us  [the longest x1 6.98 us: local(): got = lax.ppermute(sent, 'ao', SWAP)]
    pallas_call x0 -> x1, Pallas kernels: none -> 6.86 us  [tile_of(): pl.pallas_call(tile_kernel, grid=(width // rows,), out_shape=jax.ShapeDty...]
  transfers between devices with their start and end apart: 8 -> 6, of which waited for: 8 -> 5; matrix products, arithmetic and copies ran while one was open for 5% -> 1% of each run, Pallas kernels for 0% -> 0%
where the time goes in v1:
time: 136 us; the launch traced here: 135 us
  blocking collectives  57.8 us (42%)
  waiting for transfers between devices  36.7 us (27%)
  starting transfers between devices  18.6 us (14%)
  local copies, waits for them, and re-layouts  7.29 us (5%)
  Pallas kernels  6.86 us (5%)
  between operations  4.6 us (3%)
  other arithmetic  2.68 us (2%)
    all_to_all x1, blocking collectives, local(): slabs = lax.all_to_all(tile.reshape(parts, share, width), 'aux', 0, 0)  45.6 us
    ppermute x1, waiting for transfers between devices, local(): lax.ppermute(x, 'ao', r)  29.4 us
    all_to_all x1, blocking collectives, local(): cross = lax.all_to_all(flipped, 'aux', 0, 0)  12.2 us
    ppermute x3, waiting for transfers between devices, local(): lax.ppermute(theirs, 'ao', [(a, a ^ 2 << bit) for a in range(2 * CHIPS)])  7.25 us
    ppermute x1, starting transfers between devices, local(): got = lax.ppermute(sent, 'ao', SWAP)  6.98 us
    pallas_call x1, Pallas kernels, tile_of(): pl.pallas_call(tile_kernel, grid=(width // rows,), out_shape=jax.ShapeDty...  6.86 us
    ppermute x3, starting transfers between devices, local(): lax.ppermute(theirs, 'ao', [(a, a ^ 2 << bit) for a in range(2 * CHIPS)])  6.84 us
    reshape x1, local copies, waits for them, and re-layouts, local(): jnp.swapaxes(orbital_factors, 0, 1).reshape(-1, width)  3.33 us
  transfers between devices with their start and end apart: 6, of which 5 were waited for; matrix products, arithmetic and copies ran while one was open for 1% of the time, Pallas kernels for 0%

profile of v1, /device:TPU:1, one launch (start us, length us, event | category | flops | bytes accessed | tf_op | source)
XLA Modules:
  0.0 134.6 jit_solution(2991491279150649189)
XLA Ops:
  0.0 0.0 copy-start.1
  0.0 0.0 copy-start.2
  0.0 3.3 %reshape.12 = f32[1000,640]{1,0:T(8,128)S(1)} reshape(f32[500,2,640]{2,1,0:T(2,128)} %bitcast.12) | data formatting | bytes 5120000 | tf_op jit(solution)/shard_map/reshape | solution.py:95
  3.3 3.3 %collective-permute-start.35 = (f32[1000,640]{1,0:T(8,128)S(1)}, f32[1000,640]{1,0:T(8,128)}, u32[]{:S(2)}, u32[]{:S(2)}) collective-permute-start(f32[1000,640]{1,0:T(8,128)S(1)} %reshape.12), channel_id=1, source_target_pairs={{0,16},{16,0},{32,48},{48,32},{64,80},{80,64},{96,112},{112,96},{1... | collective-permute-start | bytes 7680008 | tf_op jit(solution)/shard_map/ppermute | solution.py:96
  6.7 0.0 copy-done.1
  6.7 0.6 slice_reduce_fusion
  9.9 0.0 copy-done.2
  9.9 0.6 dynamic_slice.3
  11.1 0.1 collective-permute-done.35
  11.3 0.3 broadcast_select_fusion.a_ref
  11.5 0.0 copy-start
  11.5 1.5 %copy-done = f32[1000,640]{1,0:T(8,128)} copy-done((f32[1000,640]{1,0:T(8,128)}, f32[1000,640]{1,0:T(8,128)S(1)}, u32[]{:S(2)}) %copy-start) | copy-done | bytes 2560024
  13.0 30.8 %conditional.1 = (f32[1000,640]{1,0:T(8,128)}) conditional(s32[]{:T(128)} %clamp.3, f32[1000,640]{1,0:T(8,128)S(1)} %broadcast_select_fusion.a_ref, f32[1000,640]{1,0:T(8,128)S(1)} %broadcast_select_fusion.a_ref, f32[1000,640]{1,0:T(8,128)S(1)} %broadcast_select_fusion.a_ref, ...), branch_computations={%region_2.3_spmd, %region_3.4_spmd, %region_4.5_spmd, %region_5.6_... | conditional | bytes 10240048 | solution.py:98
  13.0 1.4 %collective-permute-start.2 = (f32[1000,640]{1,0:T(8,128)S(1)}, f32[1000,640]{1,0:T(8,128)}, u32[]{:S(2)}, u32[]{:S(2)}) collective-permute-start(f32[1000,640]{1,0:T(8,128)S(1)} %param.2), channel_id=1, source_target_pairs={{48,0},{64,16},{16,32},{96,48},{112,64},{0,80},{80,96},{32,112},{1... | collective-permute-start | bytes 7680008 | tf_op jit(solution)/shard_map/cond/branch_2_fun/ppermute | solution.py:99
  14.5 29.4 %collective-permute-done.2 = f32[1000,640]{1,0:T(8,128)} collective-permute-done((f32[1000,640]{1,0:T(8,128)S(1)}, f32[1000,640]{1,0:T(8,128)}, u32[]{:S(2)}, u32[]{:S(2)}) %collective-permute-start.2) | collective-permute-done | bytes 2560032 | tf_op jit(solution)/shard_map/cond/branch_2_fun/ppermute | solution.py:99
  43.8 6.9 %shard_map.37 = f32[640,640]{1,0:T(8,128)S(1)} custom-call(f32[1000,640]{1,0:T(8,128)} %copy-done, f32[1000,640]{1,0:T(8,128)} %get-tuple-element.82.p_ref), custom_call_target="tpu_custom_call" | custom-call | tf_op jit(solution)/shard_map/pallas_call | solution.py:66
  50.7 45.6 %all_to_all.10 = f32[16,40,640]{2,1,0:T(8,128)S(1)} all-to-all(f32[16,40,640]{2,1,0:T(8,128)S(1)} %bitcast.11), channel_id=1, replica_groups=mesh['ao'=16,'aux'=16] {'aux'}, dimensions={0} | all-to-all | bytes 3276800 | tf_op jit(solution)/shard_map/all_to_all | solution.py:103
  96.3 0.1 reduce_sum.9
  96.4 0.2 copy.8
  96.6 0.3 reshape.16
  96.9 12.2 %all_to_all.11 = f32[16,1,1600]{2,1,0:T(1,128)S(1)} all-to-all(f32[16,1,1600]{2,1,0:T(1,128)S(1)} %reshape.16), channel_id=1, replica_groups=mesh['ao'=16,'aux'=16] {'aux'}, dimensions={0} | all-to-all | bytes 204800 | tf_op jit(solution)/shard_map/all_to_all | solution.py:106
  109.1 0.5 broadcast
  109.6 0.9 reduce.2
  110.5 0.2 reshape.17
  110.7 0.1 copy.7
  110.7 0.2 reshape.15
  110.9 2.7 %collective-permute-start.36 = (f32[40,640]{1,0:T(8,128)S(1)}, f32[40,640]{1,0:T(8,128)S(1)}, u32[]{:S(2)}, u32[]{:S(2)}) collective-permute-start(f32[40,640]{1,0:T(8,128)S(1)} %reshape.15), channel_id=1, source_target_pairs={{0,32},{16,48},{32,0},{48,16},{64,96},{80,112},{96,64},{112,80},{1... | collective-permute-start | bytes 307208 | tf_op jit(solution)/shard_map/ppermute | solution.py:109
  113.6 2.4 %collective-permute-done.36 = f32[40,640]{1,0:T(8,128)S(1)} collective-permute-done((f32[40,640]{1,0:T(8,128)S(1)}, f32[40,640]{1,0:T(8,128)S(1)}, u32[]{:S(2)}, u32[]{:S(2)}) %collective-permute-start.36) | collective-permute-done | bytes 102432 | tf_op jit(solution)/shard_map/ppermute | solution.py:109
  116.0 1.3 collective-permute-start.37
  117.3 2.6 %collective-permute-done.37 = f32[40,640]{1,0:T(8,128)S(1)} collective-permute-done((f32[40,640]{1,0:T(8,128)S(1)}, f32[40,640]{1,0:T(8,128)S(1)}, u32[]{:S(2)}, u32[]{:S(2)}) %collective-permute-start.37) | collective-permute-done | bytes 102432 | tf_op jit(solution)/shard_map/ppermute | solution.py:109
  119.9 2.8 %collective-permute-start.38 = (f32[40,640]{1,0:T(8,128)S(1)}, f32[40,640]{1,0:T(8,128)S(1)}, u32[]{:S(2)}, u32[]{:S(2)}) collective-permute-start(f32[40,640]{1,0:T(8,128)S(1)} %broadcast_select_fusion.3), channel_id=1, source_target_pairs={{0,128},{16,144},{32,160},{48,176},{64,192},{80,208},{96,224},{112... | collective-permute-start | bytes 307208 | tf_op jit(solution)/shard_map/ppermute | solution.py:109
  122.8 2.3 %collective-permute-done.38 = f32[40,640]{1,0:T(8,128)S(1)} collective-permute-done((f32[40,640]{1,0:T(8,128)S(1)}, f32[40,640]{1,0:T(8,128)S(1)}, u32[]{:S(2)}, u32[]{:S(2)}) %collective-permute-start.38) | collective-permute-done | bytes 102432 | tf_op jit(solution)/shard_map/ppermute | solution.py:109
  125.1 7.0 %collective-permute-start.39 = (f32[40,640]{1,0:T(8,128)S(1)}, f32[40,640]{1,0:T(8,128)S(1)}, u32[]{:S(2)}, u32[]{:S(2)}) collective-permute-start(f32[40,640]{1,0:T(8,128)S(1)} %get-tuple-element.78), channel_id=1, source_target_pairs={{0,16},{16,0},{32,48},{48,32},{64,80},{80,64},{96,112},{112,96},{1... | collective-permute-start | bytes 307208 | tf_op jit(solution)/shard_map/ppermute | solution.py:113
  132.0 0.5 slice.7
  133.8 0.0 collective-permute-done.39
  133.9 0.7 pad_maximum_fusion
  (4 shorter events, 0.1 us)
Async XLA Ops:
  0.0 6.7 %copy-start.1 = (s32[2,16]{1,0:T(2,128)S(1)}, s32[2,16]{1,0:T(2,128)}, u32[]{:S(2)}) copy-start(s32[2,16]{1,0:T(2,128)} %param.39) | copy-start | bytes 388
  0.0 9.9 %copy-start.2 = (s32[256]{0:T(256)S(1)}, s32[256]{0:T(256)}, u32[]{:S(2)}) copy-start(s32[256]{0:T(256)} %constant.29.clone) | copy-start | bytes 3076
  3.3 7.9 %collective-permute-start.35 = (f32[1000,640]{1,0:T(8,128)S(1)}, f32[1000,640]{1,0:T(8,128)}, u32[]{:S(2)}, u32[]{:S(2)}) collective-permute-start(f32[1000,640]{1,0:T(8,128)S(1)} %reshape.12), channel_id=1, source_target_pairs={{0,16},{16,0},{32,48},{48,32},{64,80},{80,64},{96,112},{112,96},{1... | collective-permute-start | bytes 7680008 | tf_op jit(solution)/shard_map/ppermute | solution.py:96
  11.5 1.5 %copy-start = (f32[1000,640]{1,0:T(8,128)}, f32[1000,640]{1,0:T(8,128)S(1)}, u32[]{:S(2)}) copy-start(f32[1000,640]{1,0:T(8,128)S(1)} %broadcast_select_fusion.a_ref) | copy-start | bytes 7680004
  13.0 30.8 %collective-permute-start.2 = (f32[1000,640]{1,0:T(8,128)S(1)}, f32[1000,640]{1,0:T(8,128)}, u32[]{:S(2)}, u32[]{:S(2)}) collective-permute-start(f32[1000,640]{1,0:T(8,128)S(1)} %param.2), channel_id=1, source_target_pairs={{48,0},{64,16},{16,32},{96,48},{112,64},{0,80},{80,96},{32,112},{1... | collective-permute-start | bytes 7680008 | tf_op jit(solution)/shard_map/cond/branch_2_fun/ppermute | solution.py:99
  110.9 5.1 %collective-permute-start.36 = (f32[40,640]{1,0:T(8,128)S(1)}, f32[40,640]{1,0:T(8,128)S(1)}, u32[]{:S(2)}, u32[]{:S(2)}) collective-permute-start(f32[40,640]{1,0:T(8,128)S(1)} %reshape.15), channel_id=1, source_target_pairs={{0,32},{16,48},{32,0},{48,16},{64,96},{80,112},{96,64},{112,80},{1... | collective-permute-start | bytes 307208 | tf_op jit(solution)/shard_map/ppermute | solution.py:109
  116.0 3.9 %collective-permute-start.37 = (f32[40,640]{1,0:T(8,128)S(1)}, f32[40,640]{1,0:T(8,128)S(1)}, u32[]{:S(2)}, u32[]{:S(2)}) collective-permute-start(f32[40,640]{1,0:T(8,128)S(1)} %broadcast_select_fusion.2), channel_id=1, source_target_pairs={{0,64},{16,80},{32,96},{48,112},{64,0},{80,16},{96,32},{112,48},{1... | collective-permute-start | bytes 307208 | tf_op jit(solution)/shard_map/ppermute | solution.py:109
  119.9 5.1 %collective-permute-start.38 = (f32[40,640]{1,0:T(8,128)S(1)}, f32[40,640]{1,0:T(8,128)S(1)}, u32[]{:S(2)}, u32[]{:S(2)}) collective-permute-start(f32[40,640]{1,0:T(8,128)S(1)} %broadcast_select_fusion.3), channel_id=1, source_target_pairs={{0,128},{16,144},{32,160},{48,176},{64,192},{80,208},{96,224},{112... | collective-permute-start | bytes 307208 | tf_op jit(solution)/shard_map/ppermute | solution.py:109
  125.1 8.8 %collective-permute-start.39 = (f32[40,640]{1,0:T(8,128)S(1)}, f32[40,640]{1,0:T(8,128)S(1)}, u32[]{:S(2)}, u32[]{:S(2)}) collective-permute-start(f32[40,640]{1,0:T(8,128)S(1)} %get-tuple-element.78), channel_id=1, source_target_pairs={{0,16},{16,0},{32,48},{48,32},{64,80},{80,64},{96,112},{112,96},{1... | collective-permute-start | bytes 307208 | tf_op jit(solution)/shard_map/ppermute | solution.py:113
